TPU v7x, 32 devices: a whole 2x2x4 slice. The times are simulated.
32 devices in a mesh: dp: 8 (over y, x, core), expert: 4 (over z).
Axes of the slice: x: 2, y: 2, z: 4, core: 2. Of those that a mesh axis runs over, the one named last changes fastest.
Arguments:
- tokens: bfloat16 [256, 4096], P(('dp', 'expert')), may hold values from -6 to 6
- expert_ids: int32 [256, 8], P(('dp', 'expert')), may hold values from 0 to 15, all different within a row; in each aligned block of 8 rows (0 to 7, 8 to 15, ...) at most 8 rows name the same one
- router: bfloat16 [16, 4096], replicated, may hold values from -0.09375 to 0.09375
- w_gate: bfloat16 [16, 1536, 4096], P('dp', 'expert'), may hold values from -0.09375 to 0.09375
- w_up: bfloat16 [16, 1536, 4096], P('dp', 'expert'), may hold values from -0.09375 to 0.09375
- w_down: bfloat16 [16, 1536, 4096], P('dp', 'expert'), may hold values from -0.15625 to 0.15625
Outputs:
- mixed: bfloat16 [256, 4096], P(('dp', 'expert'))
Inputs may be any that keep to these rules, and one draw needn't show every extreme that they name: `expert_ids`: each row names 8 different experts. Within the rows of one device (aligned blocks of 8 rows) no expert is named by more than 8 rows, and in some block one expert is named by exactly 8 rows.
All inputs are finite; a program needn't handle non-finite values.
Results may differ from a plain program's by a relative error of at most 0.0049.
Values may be sent and summed in bfloat16 or wider, within the bound.
No kernel may reach another device: no remote copies, remote signals or barrier semaphores. Data moves between devices by JAX's collectives and lax.ppermute only.
A program may use at most 192 MiB of HBM per device.

v0:
```python
import jax
import jax.numpy as jnp
from jax import lax
from jax.sharding import PartitionSpec as P


def times_rows(left, right):
    return lax.dot_general(
        left, right, (((1,), (1,)), ((), ())), preferred_element_type=jnp.float32
    )


def expert_ffn(picked_rows, gate_w, up_w, down_w):
    gate_proj = times_rows(picked_rows, gate_w)
    up_proj = times_rows(picked_rows, up_w)
    hidden = (jax.nn.silu(gate_proj) * up_proj).astype(jnp.bfloat16)
    return jnp.dot(hidden, down_w, preferred_element_type=jnp.float32)


def route_slots(group_ids, expert_total, capacity):
    group_count, tok_rows, topk_count = group_ids.shape
    flat_ids = group_ids.reshape(group_count, tok_rows * topk_count)
    onehot = (flat_ids[:, :, None] == lax.iota(jnp.int32, expert_total)[None, None, :]).astype(
        jnp.int32
    )
    before = jnp.cumsum(onehot, axis=1) - onehot
    rank_in = jnp.sum(before * onehot, axis=2)
    return (flat_ids * capacity + rank_in).reshape(group_count, tok_rows, topk_count)


def gate_weights(group_rows, group_ids, router):
    logits = jnp.einsum("gtd,ed->gte", group_rows, router, preferred_element_type=jnp.float32)
    chosen = jnp.take_along_axis(logits, group_ids, axis=2)
    scores = jax.nn.sigmoid(chosen)
    return scores / jnp.sum(scores, axis=2, keepdims=True)


def dispatch_rows(group_rows, slot_ids, slot_count):
    slot_match = slot_ids[:, None, :, :] == lax.iota(jnp.int32, slot_count)[None, :, None, None]
    placing = jnp.sum(slot_match.astype(jnp.float32), axis=3).astype(jnp.bfloat16)
    return jnp.einsum(
        "gst,gtd->gsd", placing, group_rows, preferred_element_type=jnp.float32
    ).astype(jnp.bfloat16)


def run_experts(routed, w_gate, w_up, w_down):
    lead, dp_count, exp_dev, capacity, width = routed.shape
    results = []
    for local in range(exp_dev):
        picked_rows = routed[:, :, local].reshape(lead * dp_count * capacity, width)
        expert_out = expert_ffn(picked_rows, w_gate[local], w_up[local], w_down[local])
        results.append(expert_out.reshape(lead, dp_count, capacity, width))
    return jnp.stack(results, axis=2)


def combine_picks(outputs, slot_ids, weight):
    slot_count = outputs.shape[1]
    slot_match = slot_ids[..., None] == lax.iota(jnp.int32, slot_count)[None, None, None, :]
    mixing = jnp.sum(jnp.where(slot_match, weight[..., None], 0.0), axis=2)
    return jnp.einsum(
        "gts,gsd->gtd",
        mixing,
        outputs,
        precision=lax.Precision.HIGHEST,
        preferred_element_type=jnp.float32,
    )


def body(tokens, expert_ids, router, w_gate, w_up, w_down):
    dp_count = lax.axis_size("dp")
    group_count = lax.axis_size("expert")
    exp_dev = w_gate.shape[0]
    tok_rows, width = tokens.shape
    topk_count = expert_ids.shape[1]
    expert_total = router.shape[0]
    capacity = max(2, 2 * tok_rows * topk_count // expert_total)
    slot_count = expert_total * capacity
    group_rows, group_ids = (
        lax.all_gather(tokens[None], "expert", axis=0, tiled=True),
        lax.all_gather(expert_ids[None], "expert", axis=0, tiled=True),
    )
    slot_ids = route_slots(group_ids, expert_total, capacity)
    weight = gate_weights(group_rows, group_ids, router)
    buffer = dispatch_rows(group_rows, slot_ids, slot_count).reshape(
        group_count, dp_count, exp_dev, capacity, width
    )
    routed = lax.all_to_all(buffer, "dp", split_axis=1, concat_axis=1, tiled=True)
    partial_value = run_experts(routed, w_gate, w_up, w_down)
    returned = lax.all_to_all(partial_value, "dp", split_axis=1, concat_axis=1, tiled=True)
    combined = combine_picks(returned.reshape(group_count, slot_count, width), slot_ids, weight)
    mixed = lax.psum_scatter(combined, "expert", scatter_dimension=0, tiled=True)[0]
    return mixed.astype(jnp.bfloat16)


def solution(mesh):
    in_specs = (
        P(("dp", "expert"), None),
        P(("dp", "expert"), None),
        P(),
        P("dp", "expert", None),
        P("dp", "expert", None),
        P("dp", "expert", None),
    )
    out_specs = P(("dp", "expert"), None)
    return jax.shard_map(body, mesh=mesh, in_specs=in_specs, out_specs=out_specs, check_vma=False)
```

profile of v0, /device:TPU:0, one launch (start us, length us, event | category | flops | bytes accessed | tf_op | source)
XLA Modules:
  0.0 243.9 jit_solution(1487760249409618271)
XLA Ops:
  6.5 0.0 copy-start
  6.5 15.1 %all-gather = s32[32,8]{1,0:T(8,128)S(1)} all-gather(s32[8,8]{1,0:T(8,128)} %param.7), channel_id=2, replica_groups=mesh['dp'=8,'expert'=4] {'expert'}, dimensions={0}, use_global_device_ids=true | all-gather | bytes 1280 | tf_op jit(solution)/shard_map/all_gather | solution.py:80
  21.6 0.1 eq.20
  21.7 0.1 fusion.32
  21.8 0.1 reduce_window_sum.11
  21.9 0.2 select_reduce_fusion.1
  22.1 0.1 reduce_sum.39
  22.2 0.1 convert_reduce_fusion
  22.4 14.5 %all-gather.1 = bf16[32,4096]{1,0:T(8,128)(2,1)S(1)} all-gather(bf16[8,4096]{1,0:T(8,128)(2,1)} %param.6), channel_id=3, replica_groups=mesh['dp'=8,'expert'=4] {'expert'}, dimensions={0}, use_global_device_ids=true | all-gather | bytes 327680 | tf_op jit(solution)/shard_map/all_gather | solution.py:79
  36.9 1.3 convolution_convert_fusion
  38.2 0.5 copy.16
  38.7 52.6 %all_to_all.10 = bf16[4,8,2,8,4096]{4,3,2,0,1:T(8,128)(2,1)S(1)} all-to-all(bf16[4,8,2,8,4096]{4,3,2,0,1:T(8,128)(2,1)S(1)} %copy.16), channel_id=1, replica_groups=mesh['dp'=8,'expert'=4] {'dp'}, dimensions={1} | all-to-all | bytes 8388608 | tf_op jit(solution)/shard_map/all_to_all | solution.py:87
  91.3 0.0 slice-start.2
  91.3 0.5 fusion.35
  91.8 0.0 slice-start.3
  91.8 0.1 copy.23
  91.9 0.0 slice-start.4
  91.9 0.1 copy.24
  92.1 0.8 slice-done.2
  92.9 1.4 slice-done.3
  94.2 0.0 slice-start.5
  94.2 1.3 fusion.8
  95.5 1.3 fusion.4
  96.7 0.0 slice-done.4
  96.8 0.0 slice-done.5
  96.8 0.0 slice-start
  96.8 1.3 fusion.25
  98.1 0.0 slice-start.1
  98.1 1.3 fusion.22
  99.3 0.0 slice-done
  99.4 0.5 slice-done.1
  99.9 1.3 convolution_bitcast_fusion
  101.1 1.3 convolution_bitcast_fusion.1
  102.4 1.0 pad_maximum_fusion
  103.4 3.8 %copy.19 = f32[4,8,2,8,4096]{4,3,0,2,1:T(8,128)} copy(f32[4,8,2,8,4096]{4,3,1,0,2:T(8,128)S(1)} %pad_maximum_fusion) | data formatting | bytes 16777216 | tf_op jit(solution)/shard_map/stack | solution.py:53
  107.2 4.9 %all-to-all-start.1 = ((f32[4,8,2,8,4096]{4,3,0,2,1:T(8,128)}), f32[4,8,2,8,4096]{4,3,0,2,1:T(8,128)}, u32[]{:S(2)}, u32[]{:S(2)}) async-start(f32[4,8,2,8,4096]{4,3,0,2,1:T(8,128)} %copy.19), calls=%async_computation.1 | async-start | bytes 16777216 | tf_op jit(solution)/shard_map/all_to_all | solution.py:89
  112.1 0.2 reduce-scatter.2.cloned.1.call-start
  112.4 0.1 reshape.56
  112.5 0.0 copy-done
  112.5 0.2 fusion.29
  112.7 1.9 gather_fusion
  114.6 0.1 reshape.59
  114.7 0.1 divide_reduce_fusion
  114.8 0.1 multiply_divide_fusion
  114.8 0.2 select_reduce_fusion
  115.0 91.2 %all-to-all-done.1 = f32[4,8,2,8,4096]{4,3,0,2,1:T(8,128)} async-done(((f32[4,8,2,8,4096]{4,3,0,2,1:T(8,128)}), f32[4,8,2,8,4096]{4,3,0,2,1:T(8,128)}, u32[]{:S(2)}, u32[]{:S(2)}) %all-to-all-start.1) | async-done | bytes 8388640 | tf_op jit(solution)/shard_map/all_to_all | solution.py:89
  206.2 3.9 %copy.20 = f32[4,8,2,8,4096]{4,3,2,1,0:T(8,128)S(1)} copy(f32[4,8,2,8,4096]{4,3,0,2,1:T(8,128)} %all-to-all-done.1) | data formatting | bytes 16777216 | tf_op jit(solution)/shard_map/all_to_all | solution.py:89
  210.1 4.8 %fusion.36 = f32[4,8,4096]{2,1,0:T(8,128)} fusion(f32[4,8,128]{2,1,0:T(8,128)S(1)} %select_reduce_fusion, f32[4,128,4096]{2,1,0:T(8,128)S(1)} %bitcast.82), kind=kOutput, calls=%fused_computation.46 | convolution fusion | flops 201326592 | bytes 8929280 | tf_op jit(solution)/shard_map/gts,gsd->gtd/dot_general | solution.py:60
  214.9 0.0 reduce-scatter.2.cloned.1.call-update
  214.9 20.6 %reduce-scatter.2.cloned.1.call-done = f32[1,8,4096]{2,1,0:T(8,128)} async-done(((f32[4,8,4096]{2,1,0:T(8,128)}), f32[1,8,4096]{2,1,0:T(8,128)}) %reduce-scatter.2.cloned.1.call-update) | async-done | bytes 131088 | tf_op jit(solution)/shard_map/reduce_scatter | solution.py:91
  235.5 1.5 convert_bitcast_fusion
  (5 shorter events, 0.0 us)
Async XLA Ops:
  6.5 105.9 %copy-start = (bf16[16,4096]{1,0:T(8,128)(2,1)S(1)}, bf16[16,4096]{1,0:T(8,128)(2,1)}, u32[]{:S(2)}) copy-start(bf16[16,4096]{1,0:T(8,128)(2,1)} %param.8) | copy-start | bytes 393220
  91.3 1.6 slice-start.2
  91.8 2.5 %slice-start.3 = ((s8[6291456]{0:T(1024)(128)(4,1)}), s8[4194304]{0:T(1024)(128)(4,1)S(1)}, s32[]{:S(2)}) async-start(s8[6291456]{0:T(1024)(128)(4,1)} %bitcast.92), calls=%async_computation.7 | async-start | bytes 8388608
  91.9 4.8 %slice-start.4 = ((s8[6291456]{0:T(1024)(128)(4,1)}), s8[4194304]{0:T(1024)(128)(4,1)S(1)}, s32[]{:S(2)}) async-start(s8[6291456]{0:T(1024)(128)(4,1)} %bitcast.94), calls=%async_computation.8 | async-start | bytes 8388608
  94.2 2.5 %slice-start.5 = ((s8[6291456]{0:T(1024)(128)(4,1)}), s8[2097152]{0:T(1024)(128)(4,1)S(1)}, s32[]{:S(2)}) async-start(s8[6291456]{0:T(1024)(128)(4,1)} %bitcast.94), calls=%async_computation.9 | async-start | bytes 4194304
  96.8 2.6 %slice-start = ((s8[6291456]{0:T(1024)(128)(4,1)}), s8[4194304]{0:T(1024)(128)(4,1)S(1)}, s32[]{:S(2)}) async-start(s8[6291456]{0:T(1024)(128)(4,1)} %bitcast.84), calls=%async_computation.4 | async-start | bytes 8388608
  98.1 1.8 slice-start.1
  107.2 99.0 %all-to-all-start.1 = ((f32[4,8,2,8,4096]{4,3,0,2,1:T(8,128)}), f32[4,8,2,8,4096]{4,3,0,2,1:T(8,128)}, u32[]{:S(2)}, u32[]{:S(2)}) async-start(f32[4,8,2,8,4096]{4,3,0,2,1:T(8,128)} %copy.19), calls=%async_computation.1 | async-start | bytes 16777216 | tf_op jit(solution)/shard_map/all_to_all | solution.py:89
  112.1 123.4 %reduce-scatter.2.cloned.1.call-start = ((), (), s32[]{:S(2)}) async-start(), calls=%async_computation.3 | async-start | bytes 655360 | tf_op jit(solution)/shard_map/reduce_scatter | solution.py:91
Sparse Core Ops, SparseCore 0:
  215.1 20.4 reduce-scatter.1
where the time goes:
time: 244 us
  waiting for transfers between devices  112 us (46%)
  blocking collectives  82.2 us (34%)
  local copies, waits for them, and re-layouts  13.9 us (6%)
  matrix products  13.9 us (6%)
  between operations  13.6 us (6%)
  starting transfers between devices  5.17 us (2%)
  other arithmetic  3.48 us (1%)
    all_to_all x1, waiting for transfers between devices, body(): lax.all_to_all(partial_value, 'dp', split_axis=1, concat_axis=1, tiled=True)  91.2 us
    all_to_all x1, blocking collectives, body(): lax.all_to_all(buffer, 'dp', split_axis=1, concat_axis=1, tiled=True)  52.6 us
    reduce_scatter x1, waiting for transfers between devices, body(): lax.psum_scatter(combined, 'expert', scatter_dimension=0, tiled=True)[0]  20.6 us
    all_gather x1, blocking collectives, body(): lax.all_gather(expert_ids[None], 'expert', axis=0, tiled=True)  15.1 us
    all_gather x1, blocking collectives, body(): lax.all_gather(tokens[None], 'expert', axis=0, tiled=True)  14.5 us
    dot_general x4, matrix products, times_rows(): lax.dot_general(left, right, (((1,), (1,)), ((), ())), preferred_element_...  5.05 us
    all_to_all x1, starting transfers between devices, body(): lax.all_to_all(partial_value, 'dp', split_axis=1, concat_axis=1, tiled=True)  4.95 us
  transfers between devices with their start and end apart: 2, of which 2 were waited for; matrix products, arithmetic and copies ran while one was open for 1% of the time, Pallas kernels for 0%

commit v1 on v0

v1 whole, which is shorter than its diff:
```python
import jax
import jax.numpy as jnp
from jax import lax
from jax.sharding import PartitionSpec as P

LANES = 128


def times_rows(left, right):
    return lax.dot_general(
        left, right, (((1,), (1,)), ((), ())), preferred_element_type=jnp.float32
    )


def swap(value, axis, bit):
    count = lax.axis_size(axis)
    return lax.ppermute(value, axis, [(i, i ^ (1 << bit)) for i in range(count)])


def axis_bits(axis):
    return list(range(lax.axis_size(axis).bit_length() - 1))


def routes():
    z_bits = [("expert", bit) for bit in reversed(axis_bits("expert"))]
    dp_bits = axis_bits("dp")
    core, plane = [("dp", bit) for bit in dp_bits[:1]], dp_bits[1:]
    x_bits = [("dp", bit) for bit in plane[: len(plane) // 2]]
    y_bits = [("dp", bit) for bit in plane[len(plane) // 2 :]]
    return z_bits, x_bits + y_bits, y_bits + x_bits, core[0]


def gather_rows(block):
    z_bits, first_way, second_way, core = routes()
    for step in z_bits[:-1]:
        block = jnp.concatenate([block, swap(block, *step)])
    first, second = block, swap(block, *z_bits[-1])
    for step_one, step_two in zip(first_way, second_way):
        other_first, other_second = swap(first, *step_one), swap(second, *step_two)
        first = jnp.concatenate([first, other_first])
        second = jnp.concatenate([second, other_second])
    return jnp.concatenate([first, second, swap(first, *core), swap(second, *core)])


def pass_on(part, step):
    half = part.shape[0] // 2
    return part[:half] + swap(part[half:].astype(jnp.bfloat16), *step).astype(jnp.float32)


def scatter_sums(total):
    z_bits, first_way, second_way, core = routes()
    half = total.shape[0] // 2
    quarter = half // 2
    away = total[half:].astype(jnp.bfloat16)
    first = total[:quarter] + swap(away[:quarter], *core).astype(jnp.float32)
    second = total[quarter:half] + swap(away[quarter:], *core).astype(jnp.float32)
    for step_one, step_two in zip(first_way[::-1], second_way[::-1]):
        first, second = pass_on(first, step_one), pass_on(second, step_two)
    part = jnp.concatenate([first, second])
    for step in z_bits[::-1]:
        part = pass_on(part, step)
    return part.astype(jnp.bfloat16)


def mixing_weights(tokens, ids, router):
    logits = times_rows(tokens, router)
    experts = lax.iota(jnp.int32, router.shape[0])
    chosen = jnp.any(ids[:, :, None] == experts[None, None, :], axis=1)
    scores = jnp.where(chosen, jax.nn.sigmoid(logits), 0.0)
    return scores / jnp.sum(scores, axis=1, keepdims=True)


def body(tokens, expert_ids, router, w_gate, w_up, w_down):
    exp_dev, _, width = w_gate.shape
    picks = expert_ids.shape[1]
    tags = jnp.pad(expert_ids.astype(jnp.bfloat16), ((0, 0), (0, LANES - picks)))
    packed = gather_rows(jnp.concatenate([tokens, tags], axis=1))
    rows, ids = packed[:, :width], packed[:, width : width + picks].astype(jnp.int32)
    mix = mixing_weights(rows, ids, router)
    mine = lax.dynamic_slice_in_dim(mix, lax.axis_index("dp") * exp_dev, exp_dev, axis=1)
    total = 0.0
    for local in range(exp_dev):
        gate = times_rows(rows, w_gate[local])
        up = times_rows(rows, w_up[local])
        hidden = (jax.nn.silu(gate) * up).astype(jnp.bfloat16)
        out = jnp.dot(hidden, w_down[local], preferred_element_type=jnp.float32)
        total = total + out * mine[:, local : local + 1]
    return scatter_sums(total)


def solution(mesh):
    in_specs = (
        P(("dp", "expert"), None),
        P(("dp", "expert"), None),
        P(),
        P("dp", "expert", None),
        P("dp", "expert", None),
        P("dp", "expert", None),
    )
    out_specs = P(("dp", "expert"), None)
    return jax.shard_map(body, mesh=mesh, in_specs=in_specs, out_specs=out_specs, check_vma=False)
```

time: 244 us -> 105 us (0.43)
  waiting for transfers between devices: 112 us -> 29.6 us
  blocking collectives: 82.2 us -> 0 us
  starting transfers between devices: 5.17 us -> 20.3 us
  between operations: 13.6 us -> 0.15 us
  matrix products: 13.9 us -> 23.4 us
  local copies, waits for them, and re-layouts: 13.9 us -> 22 us
  other arithmetic: 3.48 us -> 8.52 us
    all_to_all x1 -> x0, waiting for transfers between devices: 91.2 us -> none  [body(): lax.all_to_all(partial_value, 'dp', split_axis=1, concat_axis=1, tiled=True)]
    all_to_all x1 -> x0, blocking collectives: 52.6 us -> none  [body(): lax.all_to_all(buffer, 'dp', split_axis=1, concat_axis=1, tiled=True)]
    ppermute x0 -> x16, waiting for transfers between devices: none -> 29.6 us  [swap(): return lax.ppermute(value, axis, [(i, i ^ 1 << bit) for i in range(count)])]
    all_gather x2 -> x0, blocking collectives: 29.6 us -> none  [the longest x1 15.1 us: body(): lax.all_gather(expert_ids[None], 'expert', axis=0, tiled=True)]
    reduce_scatter x1 -> x0, waiting for transfers between devices: 20.6 us -> none  [body(): lax.psum_scatter(combined, 'expert', scatter_dimension=0, tiled=True)[0]]
    ppermute x0 -> x16, starting transfers between devices: none -> 20.3 us  [swap(): return lax.ppermute(value, axis, [(i, i ^ 1 << bit) for i in range(count)])]
    concatenate x0 -> x2, local copies, waits for them, and re-layouts: none -> 10.4 us  [the longest x1 8.99 us: gather_rows(): jnp.concatenate([first, second, swap(first, *core), swap(second, *core)])]
    ppermute x0 -> x8, local copies, waits for them, and re-layouts: none -> 10.2 us  [swap(): return lax.ppermute(value, axis, [(i, i ^ 1 << bit) for i in range(count)])]
  transfers between devices with their start and end apart: 2 -> 16, of which waited for: 2 -> 12; matrix products, arithmetic and copies ran while one was open for 1% -> 13% of each run, Pallas kernels for 0% -> 0%
where the time goes in v1:
time: 105 us; the launch traced here: 104 us
  waiting for transfers between devices  29.6 us (28%)
  matrix products  23.4 us (22%)
  local copies, waits for them, and re-layouts  22 us (21%)
  starting transfers between devices  20.3 us (19%)
  other arithmetic  8.52 us (8%)
    ppermute x16, waiting for transfers between devices, swap(): return lax.ppermute(value, axis, [(i, i ^ 1 << bit) for i in range(count)])  29.6 us
    ppermute x16, starting transfers between devices, swap(): return lax.ppermute(value, axis, [(i, i ^ 1 << bit) for i in range(count)])  20.3 us
    dot_general x2, matrix products, body(): out = jnp.dot(hidden, w_down[local], preferred_element_type=jnp.float32)  16.6 us
    ppermute x8, local copies, waits for them, and re-layouts, swap(): return lax.ppermute(value, axis, [(i, i ^ 1 << bit) for i in range(count)])  10.2 us
    concatenate x1, local copies, waits for them, and re-layouts, gather_rows(): jnp.concatenate([first, second, swap(first, *core), swap(second, *core)])  8.99 us
    dot_general x3, matrix products, times_rows(): lax.dot_general(left, right, (((1,), (1,)), ((), ())), preferred_element_...  6.78 us
    concatenate x2, other arithmetic, gather_rows(): first = jnp.concatenate([first, other_first])  2.57 us
  transfers between devices with their start and end apart: 16, of which 12 were waited for; matrix products, arithmetic and copies ran while one was open for 13% of the time, Pallas kernels for 0%

profile of v1, /device:TPU:0, one launch (start us, length us, event | category | flops | bytes accessed | tf_op | source)
XLA Modules:
  0.0 104.0 jit_solution(16115756112807369956)
XLA Ops:
  0.0 0.0 copy-start
  0.0 0.7 convert_element_type.50
  0.7 0.8 pad_maximum_fusion.5
  1.6 4.0 %collective-permute-start = (bf16[8,4224]{1,0:T(8,128)(2,1)S(1)}, bf16[8,4224]{1,0:T(8,128)(2,1)S(1)}, u32[]{:S(2)}, u32[]{:S(2)}) collective-permute-start(bf16[8,4224]{1,0:T(8,128)(2,1)S(1)} %pad_maximum_fusion.5), channel_id=1, source_target_pairs={{0,2},{1,3},{2,0},{3,1},{4,6},{5,7},{6,4},{7,5},{8,10},{9,11},{10,... | collective-permute-start | bytes 202760 | tf_op jit(solution)/shard_map/ppermute | solution.py:17
  5.6 3.7 %collective-permute-done = bf16[8,4224]{1,0:T(8,128)(2,1)S(1)} collective-permute-done((bf16[8,4224]{1,0:T(8,128)(2,1)S(1)}, bf16[8,4224]{1,0:T(8,128)(2,1)S(1)}, u32[]{:S(2)}, u32[]{:S(2)}) %collective-permute-start) | collective-permute-done | bytes 67616 | tf_op jit(solution)/shard_map/ppermute | solution.py:17
  9.3 0.8 pad_maximum_fusion.4
  10.2 0.7 collective-permute-start.3
  10.8 1.5 %collective-permute-start.1 = (bf16[16,4224]{1,0:T(8,128)(2,1)S(1)}, bf16[16,4224]{1,0:T(8,128)(2,1)S(1)}, u32[]{:S(2)}, u32[]{:S(2)}) collective-permute-start(bf16[16,4224]{1,0:T(8,128)(2,1)S(1)} %pad_maximum_fusion.4), channel_id=1, source_target_pairs={{0,8},{4,12},{8,0},{12,4},{16,24},{20,28},{24,16},{28,20},{1,9},{5... | collective-permute-start | bytes 405512 | tf_op jit(solution)/shard_map/ppermute | solution.py:17
  12.3 2.9 %collective-permute-done.3 = bf16[16,4224]{1,0:T(8,128)(2,1)S(1)} collective-permute-done((bf16[16,4224]{1,0:T(8,128)(2,1)S(1)}, bf16[16,4224]{1,0:T(8,128)(2,1)S(1)}, u32[]{:S(2)}, u32[]{:S(2)}) %collective-permute-start.3) | collective-permute-done | bytes 135200 | tf_op jit(solution)/shard_map/ppermute | solution.py:17
  15.3 1.7 %collective-permute-start.4 = (bf16[16,4224]{1,0:T(8,128)(2,1)S(1)}, bf16[16,4224]{1,0:T(8,128)(2,1)S(1)}, u32[]{:S(2)}, u32[]{:S(2)}) collective-permute-start(bf16[16,4224]{1,0:T(8,128)(2,1)S(1)} %collective-permute-done.3), channel_id=1, source_target_pairs={{0,16},{4,20},{8,24},{12,28},{16,0},{20,4},{24,8},{28,12},{1,17},{... | collective-permute-start | bytes 405512 | tf_op jit(solution)/shard_map/ppermute | solution.py:17
  17.0 0.0 collective-permute-done.1
  17.0 0.9 pad_maximum_fusion.2
  17.9 0.4 collective-permute-start.2
  18.3 3.4 %collective-permute-done.4 = bf16[16,4224]{1,0:T(8,128)(2,1)S(1)} collective-permute-done((bf16[16,4224]{1,0:T(8,128)(2,1)S(1)}, bf16[16,4224]{1,0:T(8,128)(2,1)S(1)}, u32[]{:S(2)}, u32[]{:S(2)}) %collective-permute-start.4) | collective-permute-done | bytes 135200 | tf_op jit(solution)/shard_map/ppermute | solution.py:17
  21.7 1.8 %collective-permute-start.5 = (bf16[32,4224]{1,0:T(8,128)(2,1)S(1)}, bf16[32,4224]{1,0:T(8,128)(2,1)S(1)}, u32[]{:S(2)}, u32[]{:S(2)}) collective-permute-start(bf16[32,4224]{1,0:T(8,128)(2,1)S(1)} %pad_maximum_fusion.3), channel_id=1, source_target_pairs={{0,8},{4,12},{8,0},{12,4},{16,24},{20,28},{24,16},{28,20},{1,9},{5... | collective-permute-start | bytes 811016 | tf_op jit(solution)/shard_map/ppermute | solution.py:17
  23.5 1.5 %collective-permute-done.2 = bf16[32,4224]{1,0:T(8,128)(2,1)S(1)} collective-permute-done((bf16[32,4224]{1,0:T(8,128)(2,1)S(1)}, bf16[32,4224]{1,0:T(8,128)(2,1)S(1)}, u32[]{:S(2)}, u32[]{:S(2)}) %collective-permute-start.2) | collective-permute-done | bytes 270368 | tf_op jit(solution)/shard_map/ppermute | solution.py:17
  25.0 1.7 %pad_maximum_fusion = bf16[64,4224]{1,0:T(8,128)(2,1)} fusion(bf16[32,4224]{1,0:T(8,128)(2,1)S(1)} %collective-permute-done.2, bf16[16,4224]{1,0:T(8,128)(2,1)S(1)} %collective-permute-done.1, bf16[8,4224]{1,0:T(8,128)(2,1)S(1)} %collective-permute-done, bf16[8,128]{1,0:T(8,128)(2,1)S(1)} %pad.4, bf16[8,4096]{1,0:T(8,128)(2,1)} %param.6), kind=kLoop, calls=%fused_computation.31 | loop fusion | flops 2703360 | bytes 1081344 | tf_op jit(solution)/shard_map/concatenate | solution.py:40
  26.7 0.0 collective-permute-start.6
  26.7 1.5 %collective-permute-done.5 = bf16[32,4224]{1,0:T(8,128)(2,1)S(1)} collective-permute-done((bf16[32,4224]{1,0:T(8,128)(2,1)S(1)}, bf16[32,4224]{1,0:T(8,128)(2,1)S(1)}, u32[]{:S(2)}, u32[]{:S(2)}) %collective-permute-start.5) | collective-permute-done | bytes 270368 | tf_op jit(solution)/shard_map/ppermute | solution.py:17
  28.3 0.9 pad_maximum_fusion.1
  29.1 0.0 collective-permute-start.7
  29.1 1.4 %copy.10 = bf16[8,4224]{0,1:T(8,128)(2,1)} copy(bf16[8,4224]{1,0:T(8,128)(2,1)S(1)} %pad_maximum_fusion.5) | data formatting | bytes 135168 | tf_op jit(solution)/shard_map/concatenate | solution.py:77
  30.5 1.4 %copy.11 = bf16[8,4224]{0,1:T(8,128)(2,1)} copy(bf16[8,4224]{1,0:T(8,128)(2,1)S(1)} %collective-permute-done) | data formatting | bytes 135168 | tf_op jit(solution)/shard_map/ppermute | solution.py:17
  31.9 0.5 copy.14
  32.4 1.4 %copy.12 = bf16[16,4224]{0,1:T(8,128)(2,1)} copy(bf16[16,4224]{1,0:T(8,128)(2,1)S(1)} %collective-permute-done.1) | data formatting | bytes 270336 | tf_op jit(solution)/shard_map/ppermute | solution.py:17
  33.8 1.4 %copy.15 = bf16[16,4224]{0,1:T(8,128)(2,1)} copy(bf16[16,4224]{1,0:T(8,128)(2,1)S(1)} %collective-permute-done.4) | data formatting | bytes 270336 | tf_op jit(solution)/shard_map/ppermute | solution.py:17
  35.2 1.4 %copy.13 = bf16[32,4224]{0,1:T(8,128)(2,1)} copy(bf16[32,4224]{1,0:T(8,128)(2,1)S(1)} %collective-permute-done.2) | data formatting | bytes 540672 | tf_op jit(solution)/shard_map/ppermute | solution.py:17
  36.5 1.4 %copy.16 = bf16[32,4224]{0,1:T(8,128)(2,1)} copy(bf16[32,4224]{1,0:T(8,128)(2,1)S(1)} %collective-permute-done.5) | data formatting | bytes 540672 | tf_op jit(solution)/shard_map/ppermute | solution.py:17
  37.9 0.0 collective-permute-done.6
  37.9 1.4 %copy.17 = bf16[64,4224]{0,1:T(8,128)(2,1)} copy(bf16[64,4224]{1,0:T(8,128)(2,1)S(1)} %collective-permute-done.6) | data formatting | bytes 1081344 | tf_op jit(solution)/shard_map/ppermute | solution.py:17
  39.3 0.0 collective-permute-done.7
  39.3 1.4 %copy.18 = bf16[64,4224]{0,1:T(8,128)(2,1)} copy(bf16[64,4224]{1,0:T(8,128)(2,1)S(1)} %collective-permute-done.7) | data formatting | bytes 1081344 | tf_op jit(solution)/shard_map/ppermute | solution.py:17
  40.7 9.0 %concatenate.31 = bf16[256,4224]{0,1:T(8,128)(2,1)S(1)} concatenate(bf16[8,4224]{0,1:T(8,128)(2,1)} %copy.10, bf16[8,4224]{0,1:T(8,128)(2,1)} %copy.11, bf16[16,4224]{0,1:T(8,128)(2,1)} %copy.12, bf16[32,4224]{0,1:T(8,128)(2,1)} %copy.13, bf16[16,4224]{0,1:T(8,128)(2,1)S(1)} %copy.14, bf16[16,4224]{0,1:T(8,128)(2,1)} %copy.15, bf16[32,4224]{0,1:T(8,128)(2,1)} %copy.16, ...), dimensions={0} | concatenate | bytes 4325376 | tf_op jit(solution)/shard_map/concatenate | solution.py:42
  49.8 3.2 %fusion.7 = f32[256,384]{1,0:T(8,128)S(1)} fusion(bf16[2,384,4096]{2,1,0:T(8,128)(2,1)} %param.10, bf16[256,4224]{0,1:T(8,128)(2,1)S(1)} %concatenate.31), kind=kOutput, calls=%fused_computation.9 | convolution fusion | flops 805306368 | bytes 5636096 | tf_op jit(solution)/shard_map/dot_general | solution.py:10
  53.0 3.2 %fusion.2 = f32[256,384]{1,0:T(8,128)S(1)} fusion(bf16[2,384,4096]{2,1,0:T(8,128)(2,1)} %param.10, bf16[256,4224]{0,1:T(8,128)(2,1)S(1)} %concatenate.31), kind=kOutput, calls=%fused_computation.4 | convolution fusion | flops 805306368 | bytes 5636096 | tf_op jit(solution)/shard_map/dot_general | solution.py:10
  56.2 0.0 copy-done
  56.2 0.4 fusion.52
  56.6 7.3 %convolution_multiply_fusion.1 = f32[256,4096]{1,0:T(8,128)} fusion(bf16[2,384,4096]{2,1,0:T(8,128)(2,1)} %param.11, f32[256]{0:T(256)S(1)} %bitcast.34, f32[256,384]{1,0:T(8,128)S(1)} %fusion.7, bf16[2,384,4096]{2,1,0:T(8,128)(2,1)} %param.9, bf16[256,4224]{0,1:T(8,128)(2,1)S(1)} %concatenate.31), kind=kOutput, calls=%fused_computation.2 | convolution fusion | flops 1612251136 | bytes 12977152 | tf_op jit(solution)/shard_map/dot_general | solution.py:86
  64.0 9.3 %fusion.53 = (bf16[256,4096]{1,0:T(8,128)(2,1)}, f32[256,4096]{1,0:T(8,128)}) fusion(f32[256,4096]{1,0:T(8,128)} %convolution_multiply_fusion.1, f32[256]{0:T(256)S(1)} %bitcast.33, bf16[2,384,4096]{2,1,0:T(8,128)(2,1)} %param.11, f32[256,384]{1,0:T(8,128)S(1)} %fusion.2, bf16[2,384,4096]{2,1,0:T(8,128)(2,1)} %param.9, bf16[256,4224]{0,1:T(8,128)(2,1)S(1)} %concatenate.31), kind=kOutput, calls=%fused_computation.63 | convolution fusion | flops 1614348288 | bytes 19268608 | tf_op jit(solution)/shard_map/dot_general | solution.py:86
  73.2 1.3 %fusion.50 = (bf16[64,4096]{1,0:T(8,128)(2,1)S(1)}, bf16[64,4096]{1,0:T(8,128)(2,1)S(1)}) fusion(bf16[256,4096]{1,0:T(8,128)(2,1)} %get-tuple-element.13), kind=kLoop, calls=%fused_computation.60 | loop fusion | bytes 2097152 | tf_op jit(solution)/shard_map/slice | solution.py:56
  74.5 0.6 collective-permute-start.11
  75.1 0.1 collective-permute-start.8
  75.1 1.5 %collective-permute-done.11 = bf16[64,4096]{1,0:T(8,128)(2,1)S(1)} collective-permute-done((bf16[64,4096]{1,0:T(8,128)(2,1)S(1)}, bf16[64,4096]{1,0:T(8,128)(2,1)S(1)}, u32[]{:S(2)}, u32[]{:S(2)}) %collective-permute-start.11) | collective-permute-done | bytes 524320 | tf_op jit(solution)/shard_map/ppermute | solution.py:17
  76.6 0.7 collective-permute-done.8
  77.3 1.8 %slice_add_fusion = (f32[64,4096]{1,0:T(8,128)S(1)}, f32[64,4096]{1,0:T(8,128)S(1)}) fusion(f32[256,4096]{1,0:T(8,128)} %get-tuple-element.14, bf16[64,4096]{1,0:T(8,128)(2,1)S(1)} %collective-permute-done.11, bf16[64,4096]{1,0:T(8,128)(2,1)S(1)} %collective-permute-done.8), kind=kLoop, calls=%fused_computation.29 | loop fusion | flops 1048576 | bytes 5242880 | tf_op jit(solution)/shard_map/add | solution.py:56
  79.2 1.8 %collective-permute-start.12 = (bf16[32,4096]{1,0:T(8,128)(2,1)S(1)}, bf16[32,4096]{1,0:T(8,128)(2,1)S(1)}, u32[]{:S(2)}, u32[]{:S(2)}) collective-permute-start(bf16[32,4096]{1,0:T(8,128)(2,1)S(1)} %slice.192), channel_id=1, source_target_pairs={{0,8},{4,12},{8,0},{12,4},{16,24},{20,28},{24,16},{28,20},{1,9},{5... | collective-permute-start | bytes 786440 | tf_op jit(solution)/shard_map/ppermute | solution.py:17
  81.0 1.6 %collective-permute-start.9 = (bf16[32,4096]{1,0:T(8,128)(2,1)S(1)}, bf16[32,4096]{1,0:T(8,128)(2,1)S(1)}, u32[]{:S(2)}, u32[]{:S(2)}) collective-permute-start(bf16[32,4096]{1,0:T(8,128)(2,1)S(1)} %slice.193), channel_id=1, source_target_pairs={{0,16},{4,20},{8,24},{12,28},{16,0},{20,4},{24,8},{28,12},{1,17},{... | collective-permute-start | bytes 786440 | tf_op jit(solution)/shard_map/ppermute | solution.py:17
  82.6 5.2 %collective-permute-done.12 = bf16[32,4096]{1,0:T(8,128)(2,1)S(1)} collective-permute-done((bf16[32,4096]{1,0:T(8,128)(2,1)S(1)}, bf16[32,4096]{1,0:T(8,128)(2,1)S(1)}, u32[]{:S(2)}, u32[]{:S(2)}) %collective-permute-start.12) | collective-permute-done | bytes 262176 | tf_op jit(solution)/shard_map/ppermute | solution.py:17
  87.8 0.1 slice_add_fusion.2
  87.9 1.8 %collective-permute-start.13 = (bf16[16,4096]{1,0:T(8,128)(2,1)S(1)}, bf16[16,4096]{1,0:T(8,128)(2,1)S(1)}, u32[]{:S(2)}, u32[]{:S(2)}) collective-permute-start(bf16[16,4096]{1,0:T(8,128)(2,1)S(1)} %slice.194), channel_id=1, source_target_pairs={{0,16},{4,20},{8,24},{12,28},{16,0},{20,4},{24,8},{28,12},{1,17},{... | collective-permute-start | bytes 393224 | tf_op jit(solution)/shard_map/ppermute | solution.py:17
  89.7 0.0 collective-permute-done.9
  89.7 0.1 slice_add_fusion.3
  89.8 1.6 %collective-permute-start.10 = (bf16[16,4096]{1,0:T(8,128)(2,1)S(1)}, bf16[16,4096]{1,0:T(8,128)(2,1)S(1)}, u32[]{:S(2)}, u32[]{:S(2)}) collective-permute-start(bf16[16,4096]{1,0:T(8,128)(2,1)S(1)} %slice.195), channel_id=1, source_target_pairs={{0,8},{4,12},{8,0},{12,4},{16,24},{20,28},{24,16},{28,20},{1,9},{5... | collective-permute-start | bytes 393224 | tf_op jit(solution)/shard_map/ppermute | solution.py:17
  91.4 1.6 %collective-permute-done.13 = bf16[16,4096]{1,0:T(8,128)(2,1)S(1)} collective-permute-done((bf16[16,4096]{1,0:T(8,128)(2,1)S(1)}, bf16[16,4096]{1,0:T(8,128)(2,1)S(1)}, u32[]{:S(2)}, u32[]{:S(2)}) %collective-permute-start.13) | collective-permute-done | bytes 131104 | tf_op jit(solution)/shard_map/ppermute | solution.py:17
  93.0 0.6 collective-permute-start.14
  93.6 1.3 %collective-permute-done.10 = bf16[16,4096]{1,0:T(8,128)(2,1)S(1)} collective-permute-done((bf16[16,4096]{1,0:T(8,128)(2,1)S(1)}, bf16[16,4096]{1,0:T(8,128)(2,1)S(1)}, u32[]{:S(2)}, u32[]{:S(2)}) %collective-permute-start.10) | collective-permute-done | bytes 131104 | tf_op jit(solution)/shard_map/ppermute | solution.py:17
  94.9 3.2 %collective-permute-done.14 = bf16[16,4096]{1,0:T(8,128)(2,1)S(1)} collective-permute-done((bf16[16,4096]{1,0:T(8,128)(2,1)S(1)}, bf16[16,4096]{1,0:T(8,128)(2,1)S(1)}, u32[]{:S(2)}, u32[]{:S(2)}) %collective-permute-start.14) | collective-permute-done | bytes 131104 | tf_op jit(solution)/shard_map/ppermute | solution.py:17
  98.1 2.2 %collective-permute-start.15 = (bf16[8,4096]{1,0:T(8,128)(2,1)S(1)}, bf16[8,4096]{1,0:T(8,128)(2,1)S(1)}, u32[]{:S(2)}, u32[]{:S(2)}) collective-permute-start(bf16[8,4096]{1,0:T(8,128)(2,1)S(1)} %slice.196), channel_id=1, source_target_pairs={{0,2},{1,3},{2,0},{3,1},{4,6},{5,7},{6,4},{7,5},{8,10},{9,11},{10,... | collective-permute-start | bytes 196616 | tf_op jit(solution)/shard_map/ppermute | solution.py:17
  100.3 3.1 %collective-permute-done.15 = bf16[8,4096]{1,0:T(8,128)(2,1)S(1)} collective-permute-done((bf16[8,4096]{1,0:T(8,128)(2,1)S(1)}, bf16[8,4096]{1,0:T(8,128)(2,1)S(1)}, u32[]{:S(2)}, u32[]{:S(2)}) %collective-permute-start.15) | collective-permute-done | bytes 65568 | tf_op jit(solution)/shard_map/ppermute | solution.py:17
  103.3 0.6 fusion.46
  (13 shorter events, 0.2 us)
Async XLA Ops:
  0.0 56.2 %copy-start = (bf16[16,4096]{1,0:T(8,128)(2,1)S(1)}, bf16[16,4096]{1,0:T(8,128)(2,1)}, u32[]{:S(2)}) copy-start(bf16[16,4096]{1,0:T(8,128)(2,1)} %param.8) | copy-start | bytes 393220
  1.6 7.7 %collective-permute-start = (bf16[8,4224]{1,0:T(8,128)(2,1)S(1)}, bf16[8,4224]{1,0:T(8,128)(2,1)S(1)}, u32[]{:S(2)}, u32[]{:S(2)}) collective-permute-start(bf16[8,4224]{1,0:T(8,128)(2,1)S(1)} %pad_maximum_fusion.5), channel_id=1, source_target_pairs={{0,2},{1,3},{2,0},{3,1},{4,6},{5,7},{6,4},{7,5},{8,10},{9,11},{10,... | collective-permute-start | bytes 202760 | tf_op jit(solution)/shard_map/ppermute | solution.py:17
  10.2 5.1 %collective-permute-start.3 = (bf16[16,4224]{1,0:T(8,128)(2,1)S(1)}, bf16[16,4224]{1,0:T(8,128)(2,1)S(1)}, u32[]{:S(2)}, u32[]{:S(2)}) collective-permute-start(bf16[16,4224]{1,0:T(8,128)(2,1)S(1)} %pad_maximum_fusion.4), channel_id=1, source_target_pairs={{0,1},{1,0},{2,3},{3,2},{4,5},{5,4},{6,7},{7,6},{8,9},{9,8},{10,11... | collective-permute-start | bytes 405512 | tf_op jit(solution)/shard_map/ppermute | solution.py:17
  10.8 6.2 %collective-permute-start.1 = (bf16[16,4224]{1,0:T(8,128)(2,1)S(1)}, bf16[16,4224]{1,0:T(8,128)(2,1)S(1)}, u32[]{:S(2)}, u32[]{:S(2)}) collective-permute-start(bf16[16,4224]{1,0:T(8,128)(2,1)S(1)} %pad_maximum_fusion.4), channel_id=1, source_target_pairs={{0,8},{4,12},{8,0},{12,4},{16,24},{20,28},{24,16},{28,20},{1,9},{5... | collective-permute-start | bytes 405512 | tf_op jit(solution)/shard_map/ppermute | solution.py:17
  15.3 6.5 %collective-permute-start.4 = (bf16[16,4224]{1,0:T(8,128)(2,1)S(1)}, bf16[16,4224]{1,0:T(8,128)(2,1)S(1)}, u32[]{:S(2)}, u32[]{:S(2)}) collective-permute-start(bf16[16,4224]{1,0:T(8,128)(2,1)S(1)} %collective-permute-done.3), channel_id=1, source_target_pairs={{0,16},{4,20},{8,24},{12,28},{16,0},{20,4},{24,8},{28,12},{1,17},{... | collective-permute-start | bytes 405512 | tf_op jit(solution)/shard_map/ppermute | solution.py:17
  17.9 7.2 %collective-permute-start.2 = (bf16[32,4224]{1,0:T(8,128)(2,1)S(1)}, bf16[32,4224]{1,0:T(8,128)(2,1)S(1)}, u32[]{:S(2)}, u32[]{:S(2)}) collective-permute-start(bf16[32,4224]{1,0:T(8,128)(2,1)S(1)} %pad_maximum_fusion.2), channel_id=1, source_target_pairs={{0,16},{4,20},{8,24},{12,28},{16,0},{20,4},{24,8},{28,12},{1,17},{... | collective-permute-start | bytes 811016 | tf_op jit(solution)/shard_map/ppermute | solution.py:17
  21.7 6.5 %collective-permute-start.5 = (bf16[32,4224]{1,0:T(8,128)(2,1)S(1)}, bf16[32,4224]{1,0:T(8,128)(2,1)S(1)}, u32[]{:S(2)}, u32[]{:S(2)}) collective-permute-start(bf16[32,4224]{1,0:T(8,128)(2,1)S(1)} %pad_maximum_fusion.3), channel_id=1, source_target_pairs={{0,8},{4,12},{8,0},{12,4},{16,24},{20,28},{24,16},{28,20},{1,9},{5... | collective-permute-start | bytes 811016 | tf_op jit(solution)/shard_map/ppermute | solution.py:17
  26.7 11.2 %collective-permute-start.6 = (bf16[64,4224]{1,0:T(8,128)(2,1)}, bf16[64,4224]{1,0:T(8,128)(2,1)S(1)}, u32[]{:S(2)}, u32[]{:S(2)}) collective-permute-start(bf16[64,4224]{1,0:T(8,128)(2,1)} %pad_maximum_fusion), channel_id=1, source_target_pairs={{0,4},{4,0},{8,12},{12,8},{16,20},{20,16},{24,28},{28,24},{1,5},{5... | collective-permute-start | bytes 1622024 | tf_op jit(solution)/shard_map/ppermute | solution.py:17
  29.1 10.2 %collective-permute-start.7 = (bf16[64,4224]{1,0:T(8,128)(2,1)}, bf16[64,4224]{1,0:T(8,128)(2,1)S(1)}, u32[]{:S(2)}, u32[]{:S(2)}) collective-permute-start(bf16[64,4224]{1,0:T(8,128)(2,1)} %pad_maximum_fusion.1), channel_id=1, source_target_pairs={{0,4},{4,0},{8,12},{12,8},{16,20},{20,16},{24,28},{28,24},{1,5},{5... | collective-permute-start | bytes 1622024 | tf_op jit(solution)/shard_map/ppermute | solution.py:17
  74.5 2.1 %collective-permute-start.11 = (bf16[64,4096]{1,0:T(8,128)(2,1)S(1)}, bf16[64,4096]{1,0:T(8,128)(2,1)S(1)}, u32[]{:S(2)}, u32[]{:S(2)}) collective-permute-start(bf16[64,4096]{1,0:T(8,128)(2,1)S(1)} %get-tuple-element.7), channel_id=1, source_target_pairs={{0,4},{4,0},{8,12},{12,8},{16,20},{20,16},{24,28},{28,24},{1,5},{5... | collective-permute-start | bytes 1572872 | tf_op jit(solution)/shard_map/ppermute | solution.py:17
  75.1 2.3 %collective-permute-start.8 = (bf16[64,4096]{1,0:T(8,128)(2,1)S(1)}, bf16[64,4096]{1,0:T(8,128)(2,1)S(1)}, u32[]{:S(2)}, u32[]{:S(2)}) collective-permute-start(bf16[64,4096]{1,0:T(8,128)(2,1)S(1)} %get-tuple-element.8), channel_id=1, source_target_pairs={{0,4},{4,0},{8,12},{12,8},{16,20},{20,16},{24,28},{28,24},{1,5},{5... | collective-permute-start | bytes 1572872 | tf_op jit(solution)/shard_map/ppermute | solution.py:17
  79.2 8.7 %collective-permute-start.12 = (bf16[32,4096]{1,0:T(8,128)(2,1)S(1)}, bf16[32,4096]{1,0:T(8,128)(2,1)S(1)}, u32[]{:S(2)}, u32[]{:S(2)}) collective-permute-start(bf16[32,4096]{1,0:T(8,128)(2,1)S(1)} %slice.192), channel_id=1, source_target_pairs={{0,8},{4,12},{8,0},{12,4},{16,24},{20,28},{24,16},{28,20},{1,9},{5... | collective-permute-start | bytes 786440 | tf_op jit(solution)/shard_map/ppermute | solution.py:17
  81.0 8.7 %collective-permute-start.9 = (bf16[32,4096]{1,0:T(8,128)(2,1)S(1)}, bf16[32,4096]{1,0:T(8,128)(2,1)S(1)}, u32[]{:S(2)}, u32[]{:S(2)}) collective-permute-start(bf16[32,4096]{1,0:T(8,128)(2,1)S(1)} %slice.193), channel_id=1, source_target_pairs={{0,16},{4,20},{8,24},{12,28},{16,0},{20,4},{24,8},{28,12},{1,17},{... | collective-permute-start | bytes 786440 | tf_op jit(solution)/shard_map/ppermute | solution.py:17
  87.9 5.0 %collective-permute-start.13 = (bf16[16,4096]{1,0:T(8,128)(2,1)S(1)}, bf16[16,4096]{1,0:T(8,128)(2,1)S(1)}, u32[]{:S(2)}, u32[]{:S(2)}) collective-permute-start(bf16[16,4096]{1,0:T(8,128)(2,1)S(1)} %slice.194), channel_id=1, source_target_pairs={{0,16},{4,20},{8,24},{12,28},{16,0},{20,4},{24,8},{28,12},{1,17},{... | collective-permute-start | bytes 393224 | tf_op jit(solution)/shard_map/ppermute | solution.py:17
  89.8 5.0 %collective-permute-start.10 = (bf16[16,4096]{1,0:T(8,128)(2,1)S(1)}, bf16[16,4096]{1,0:T(8,128)(2,1)S(1)}, u32[]{:S(2)}, u32[]{:S(2)}) collective-permute-start(bf16[16,4096]{1,0:T(8,128)(2,1)S(1)} %slice.195), channel_id=1, source_target_pairs={{0,8},{4,12},{8,0},{12,4},{16,24},{20,28},{24,16},{28,20},{1,9},{5... | collective-permute-start | bytes 393224 | tf_op jit(solution)/shard_map/ppermute | solution.py:17
  93.0 5.0 %collective-permute-start.14 = (bf16[16,4096]{1,0:T(8,128)(2,1)S(1)}, bf16[16,4096]{1,0:T(8,128)(2,1)S(1)}, u32[]{:S(2)}, u32[]{:S(2)}) collective-permute-start(bf16[16,4096]{1,0:T(8,128)(2,1)S(1)} %fusion.26), channel_id=1, source_target_pairs={{0,1},{1,0},{2,3},{3,2},{4,5},{5,4},{6,7},{7,6},{8,9},{9,8},{10,11... | collective-permute-start | bytes 393224 | tf_op jit(solution)/shard_map/ppermute | solution.py:17
  98.1 5.2 %collective-permute-start.15 = (bf16[8,4096]{1,0:T(8,128)(2,1)S(1)}, bf16[8,4096]{1,0:T(8,128)(2,1)S(1)}, u32[]{:S(2)}, u32[]{:S(2)}) collective-permute-start(bf16[8,4096]{1,0:T(8,128)(2,1)S(1)} %slice.196), channel_id=1, source_target_pairs={{0,2},{1,3},{2,0},{3,1},{4,6},{5,7},{6,4},{7,5},{8,10},{9,11},{10,... | collective-permute-start | bytes 196616 | tf_op jit(solution)/shard_map/ppermute | solution.py:17
